TPU v7x, 512 devices: a whole 4x4x16 slice. The times are simulated.
512 devices in a mesh: seq: 128 (over z, x, core), head: 4 (over y).
Axes of the slice: x: 4, y: 4, z: 16, core: 2. Of those that a mesh axis runs over, the one named last changes fastest.
Arguments:
- queries: bfloat16 [32768, 4096], P('seq', 'head'), may hold values from -100 to 100
- keys_values: bfloat16 [32768, 2, 512], P('seq', None, 'head'), may hold values from -4.5 to 4.5
- cache_kv: bfloat16 [32768, 2, 512], P('seq', None, 'head'), may hold values from -4 to 4
- vertical_pages: int32 [4, 4], P('head'), may hold values from 0 to 255, as said below
- slash_shift: int32 [4, 3], P('head'), may hold values from 1 to 128, as said below
- slash_live: int32 [128, 4, 3], P('seq', 'head'), may hold values 0 or 1
- out_proj: bfloat16 [4096, 2048], P('head'), may hold values from -0.09375 to 0.09375
Outputs:
- projected: bfloat16 [32768, 2048], P('seq', 'head')
Inputs may be any that keep to these rules, and one draw needn't show every extreme that they name: `vertical_pages`: each head group lists 4 distinct pages. `slash_shift`: each head group lists 3 distinct distances.
All inputs are finite; a program needn't handle non-finite values. No bound on the sum of `slash_live` on one device may be relied on, other than what follows from the above.
Results may differ from a plain program's by a relative error of at most 0.0057.
Values may be sent and summed in bfloat16 or wider, within the bound.
A program may use at most 64 MiB of HBM per device.

v0:
```python
import jax
import jax.numpy as jnp
from jax import lax
from jax.sharding import PartitionSpec as P

PAGE = 128


def passed_along(value, axis, steps):
    count = lax.axis_size(axis)
    pairs = [(source, (source + steps) % count) for source in range(count)]
    return lax.ppermute(value, axis, pairs)


def broadcast(value, axis, source):
    kept = jnp.where(lax.axis_index(axis) == source, value, 0).astype(value.dtype)
    return lax.psum(kept, axis)


def rotate(stacked, amounts, shards):
    reduced = amounts % shards
    for bit_number in range(max(1, (shards - 1).bit_length())):
        moved = passed_along(stacked, "seq", 1 << bit_number)
        chosen = reduced // (1 << bit_number) % 2 == 1
        stacked = jnp.where(chosen[:, None, None, None], moved, stacked)
    return stacked


def body(queries, keys_values, cache_kv, vertical_pages, slash_shift, slash_live, out_proj):
    row_count = queries.shape[0]
    head_width = keys_values.shape[2]
    group_heads = queries.shape[1] // head_width
    shards = lax.axis_size("seq")
    own_shard = lax.axis_index("seq")
    distances = slash_shift[0]
    live_blocks = slash_live[0, 0] == 1
    page_ids = vertical_pages[0]
    slash_count = distances.shape[0]
    payload = jnp.where(
        (own_shard < shards - distances)[:, None, None, None], keys_values[None], cache_kv[None]
    )
    slash_kv = jnp.concatenate(
        [
            rotate(payload[position : position + 1], distances[position : position + 1], shards)
            for position in range(slash_count)
        ],
        0,
    )
    per_shard = row_count // PAGE
    owners = page_ids // per_shard
    offsets = page_ids % per_shard * PAGE
    copies = []
    for position in range(page_ids.shape[0]):
        own_page = lax.dynamic_slice_in_dim(cache_kv, offsets[position], PAGE, 0)
        copies.append(broadcast(own_page, "seq", owners[position]))
    vertical = jnp.stack(copies, 0)
    cached_slash = own_shard + shards - distances
    clash = (
        live_blocks[None, :]
        & (distances[None, :] > own_shard)
        & (owners[:, None] == cached_slash[None, :])
    )
    page_open = jnp.logical_not(jnp.any(clash, axis=1))
    row_ids = lax.broadcasted_iota(jnp.int32, (row_count, row_count), 0)
    col_ids = lax.broadcasted_iota(jnp.int32, (row_count, row_count), 1)
    causal = row_ids >= col_ids
    column_open = jnp.concatenate([jnp.repeat(live_blocks, row_count), jnp.repeat(page_open, PAGE)])
    visible = jnp.concatenate(
        [causal, jnp.broadcast_to(column_open[None, :], (row_count, column_open.shape[0]))], 1
    )
    all_keys = jnp.concatenate(
        [keys_values, slash_kv.reshape(-1, 2, head_width), vertical.reshape(-1, 2, head_width)], 0
    )
    query_heads = queries.reshape(row_count, group_heads, head_width)
    scores = jnp.einsum(
        "rgd,kd->grk", query_heads, all_keys[:, 0, :], preferred_element_type=jnp.float32
    )
    scores = scores * head_width ** (-0.5)
    scores = jnp.where(visible[None], scores, -jnp.inf)
    row_max = jnp.max(scores, axis=2, keepdims=True)
    weights = jnp.exp(scores - row_max)
    row_total = jnp.sum(weights, axis=2, keepdims=True)
    weights_bf = (weights / row_total).astype(jnp.bfloat16)
    attended = jnp.einsum(
        "grk,kd->rgd", weights_bf, all_keys[:, 1, :], preferred_element_type=jnp.float32
    )
    attended = attended.astype(jnp.bfloat16).reshape(row_count, group_heads * head_width)
    group_terms = jnp.dot(attended, out_proj, preferred_element_type=jnp.float32)
    return lax.psum_scatter(group_terms, "head", scatter_dimension=1, tiled=True).astype(
        jnp.bfloat16
    )


def solution(mesh):
    placed = (
        P("seq", "head"),
        P("seq", None, "head"),
        P("seq", None, "head"),
        P("head", None),
        P("head", None),
        P("seq", "head", None),
        P("head", None),
    )
    return jax.shard_map(
        body, mesh=mesh, in_specs=placed, out_specs=P("seq", "head"), check_vma=False
    )
```

profile of v0, /device:TPU:1, one launch (start us, length us, event | category | flops | bytes accessed | tf_op | source)
XLA Modules:
  0.0 558.2 jit_solution(9154548821410170501)
XLA Ops:
  6.5 1.0 copy.18
  7.5 0.9 copy.16
  8.5 0.7 compare_bitcast_fusion
  9.1 0.1 broadcast_select_fusion
  9.3 4.5 collective-permute-start
  13.8 1.9 collective-permute-start.14
  15.7 3.5 collective-permute-start.7
  19.2 0.7 fusion.25
  19.9 0.7 fusion.30
  30.8 1.8 fusion.20
  32.6 0.0 reduce-scatter.2.cloned.1.call-start
  32.7 0.7 compare_bitcast_fusion.1
  33.4 0.7 subtract_bitcast_fusion
  34.1 0.1 broadcast_in_dim.281
  34.1 0.2 and_reduce_fusion
  34.3 0.1 broadcast_bitcast_fusion
  34.4 0.3 pad_add_fusion
  34.7 1.4 fusion.29
  42.1 2.8 collective-permute-start.1
  45.3 319.2 %all-reduce.3.cloned.1.call-done = (bf16[1,128,2,128]{3,2,1,0:T(2,128)(2,1)}, bf16[1,128,2,128]{3,2,1,0:T(2,128)(2,1)}, bf16[1,128,2,128]{3,2,1,0:T(2,128)(2,1)}, bf16[1,128,2,128]{3,2,1,0:T(2,128)(2,1)}) async-done(((bf16[1,128,2,128]{3,2,1,0:T(2,128)(2,1)}, bf16[1,128,2,128]{3,2,1,0:T(2,128)(2,1)}, bf16[1,128,2,128]{3,2,1,0:T(2,128)(2,1)}, bf16[1,128,2,128]{3,2,1,0:T(2,128)(2,1)}), ...) | async-done | bytes 262160 | tf_op jit(solution)/shard_map/psum | solution.py:17
  364.5 1.4 pad_maximum_fusion.2
  365.9 2.8 collective-permute-start.8
  368.7 2.4 collective-permute-start.15
  371.2 4.5 collective-permute-start.2
  375.7 2.0 collective-permute-start.9
  377.6 0.8 collective-permute-done.15
  378.5 4.4 collective-permute-start.16
  382.9 4.2 collective-permute-start.3
  387.2 1.9 collective-permute-start.10
  389.2 2.7 collective-permute-start.17
  391.9 5.5 collective-permute-start.4
  397.4 2.6 collective-permute-start.11
  400.0 3.9 collective-permute-start.18
  404.0 3.9 collective-permute-start.5
  407.9 6.1 %collective-permute-start.12 = (bf16[1,256,2,128]{3,1,0,2:T(8,128)(2,1)S(1)}, bf16[1,256,2,128]{3,1,0,2:T(8,128)(2,1)S(1)}, u32[]{:S(2)}, u32[]{:S(2)}) collective-permute-start(bf16[1,256,2,128]{3,1,0,2:T(8,128)(2,1)S(1)} %broadcast_select_fusion.16), channel_id=1, source_target_pairs={{0,128},{4,132},{8,136},{12,140},{16,144},{20,148},{24,152},{28,15... | collective-permute-start | bytes 393224 | tf_op jit(solution)/shard_map/ppermute | solution.py:12
  414.0 4.2 collective-permute-start.19
  418.3 8.7 %collective-permute-start.6 = (bf16[1,256,2,128]{3,1,0,2:T(8,128)(2,1)S(1)}, bf16[1,256,2,128]{3,1,0,2:T(8,128)(2,1)S(1)}, u32[]{:S(2)}, u32[]{:S(2)}) collective-permute-start(bf16[1,256,2,128]{3,1,0,2:T(8,128)(2,1)S(1)} %broadcast_select_fusion.24), channel_id=1, source_target_pairs={{0,256},{4,260},{8,264},{12,268},{16,272},{20,276},{24,280},{28,28... | collective-permute-start | bytes 393224 | tf_op jit(solution)/shard_map/ppermute | solution.py:12
  427.0 5.3 collective-permute-start.13
  432.4 8.7 %collective-permute-start.20 = (bf16[1,256,2,128]{3,1,0,2:T(8,128)(2,1)S(1)}, bf16[1,256,2,128]{3,1,0,2:T(8,128)(2,1)S(1)}, u32[]{:S(2)}, u32[]{:S(2)}) collective-permute-start(bf16[1,256,2,128]{3,1,0,2:T(8,128)(2,1)S(1)} %broadcast_select_fusion.10), channel_id=1, source_target_pairs={{0,256},{4,260},{8,264},{12,268},{16,272},{20,276},{24,280},{28,28... | collective-permute-start | bytes 393224 | tf_op jit(solution)/shard_map/ppermute | solution.py:12
  441.1 10.1 %collective-permute-done.13 = bf16[1,256,2,128]{3,1,0,2:T(8,128)(2,1)S(1)} collective-permute-done((bf16[1,256,2,128]{3,1,0,2:T(8,128)(2,1)S(1)}, bf16[1,256,2,128]{3,1,0,2:T(8,128)(2,1)S(1)}, u32[]{:S(2)}, u32[]{:S(2)}) %collective-permute-start.13) | collective-permute-done | bytes 131104 | tf_op jit(solution)/shard_map/ppermute | solution.py:12
  451.2 10.7 %collective-permute-done.20 = bf16[1,256,2,128]{3,1,0,2:T(8,128)(2,1)S(1)} collective-permute-done((bf16[1,256,2,128]{3,1,0,2:T(8,128)(2,1)S(1)}, bf16[1,256,2,128]{3,1,0,2:T(8,128)(2,1)S(1)}, u32[]{:S(2)}, u32[]{:S(2)}) %collective-permute-start.20) | collective-permute-done | bytes 131104 | tf_op jit(solution)/shard_map/ppermute | solution.py:12
  461.9 0.1 pad_maximum_fusion
  462.0 6.9 %fusion.32 = (f32[8,256]{1,0:T(8,128)S(1)}, f32[8,256,1536]{1,2,0:T(8,128)}) fusion(pred[256,1536]{0,1:T(8,128)(4,1)S(1)} %pad_add_fusion, bf16[1536,2,128]{2,0,1:T(8,128)(2,1)S(1)} %pad_maximum_fusion, bf16[256,1024]{1,0:T(8,128)(2,1)S(1)} %copy-done), kind=kOutput, calls=%fused_computation.74 | convolution fusion | flops 817890816 | bytes 13901824 | tf_op jit(solution)/shard_map/sub | solution.py:81
  468.9 5.7 %fusion.8 = bf16[128,8,256]{2,0,1:T(8,128)(2,1)S(1)} fusion(f32[8,256,1536]{1,2,0:T(8,128)} %get-tuple-element.35, f32[8,256]{1,0:T(8,128)S(1)} %get-tuple-element.34, bf16[1536,2,128]{2,0,1:T(8,128)(2,1)S(1)} %pad_maximum_fusion), kind=kOutput, calls=%fused_computation.11 | convolution fusion | flops 811859968 | bytes 13508608 | tf_op jit(solution)/shard_map/grk,kd->rgd/dot_general | solution.py:84
  474.6 0.0 copy-done.1
  474.7 2.6 fusion.37
  477.3 72.3 %reduce-scatter.2.cloned.1.call-done = f32[256,512]{1,0:T(8,128)} async-done(((f32[256,2048]{1,0:T(8,128)}), f32[256,512]{1,0:T(8,128)}) %reduce-scatter.2.cloned.1.call-update) | async-done | bytes 524304 | tf_op jit(solution)/shard_map/reduce_scatter | solution.py:89
  549.6 1.8 convert_element_type.20
  (51 shorter events, 0.6 us)
Async XLA Ops:
  6.5 455.4 %copy-start = (bf16[256,1024]{1,0:T(8,128)(2,1)S(1)}, bf16[256,1024]{1,0:T(8,128)(2,1)}, u32[]{:S(2)}) copy-start(bf16[256,1024]{1,0:T(8,128)(2,1)} %param.7) | copy-start | bytes 1572868
  6.5 357.9 %all-reduce.3.cloned.1.call-start = ((), (), s32[]{:S(2)}) async-start(), calls=%async_computation.2 | async-start | bytes 524288 | tf_op jit(solution)/shard_map/psum | solution.py:17
  9.3 32.7 %collective-permute-start = (bf16[1,256,2,128]{3,1,0,2:T(8,128)(2,1)S(1)}, bf16[1,256,2,128]{3,1,0,2:T(8,128)(2,1)S(1)}, u32[]{:S(2)}, u32[]{:S(2)}) collective-permute-start(bf16[1,256,2,128]{3,1,0,2:T(8,128)(2,1)S(1)} %get-tuple-element.12), channel_id=1, source_target_pairs={{0,4},{4,8},{8,12},{12,16},{16,20},{20,24},{24,28},{28,32},{32,36}... | collective-permute-start | bytes 393224 | tf_op jit(solution)/shard_map/ppermute | solution.py:12
  13.8 28.2 %collective-permute-start.14 = (bf16[1,256,2,128]{3,1,0,2:T(8,128)(2,1)S(1)}, bf16[1,256,2,128]{3,1,0,2:T(8,128)(2,1)S(1)}, u32[]{:S(2)}, u32[]{:S(2)}) collective-permute-start(bf16[1,256,2,128]{3,1,0,2:T(8,128)(2,1)S(1)} %get-tuple-element.13), channel_id=1, source_target_pairs={{0,4},{4,8},{8,12},{12,16},{16,20},{20,24},{24,28},{28,32},{32,36}... | collective-permute-start | bytes 393224 | tf_op jit(solution)/shard_map/ppermute | solution.py:12
  15.7 26.3 %collective-permute-start.7 = (bf16[1,256,2,128]{3,1,0,2:T(8,128)(2,1)S(1)}, bf16[1,256,2,128]{3,1,0,2:T(8,128)(2,1)S(1)}, u32[]{:S(2)}, u32[]{:S(2)}) collective-permute-start(bf16[1,256,2,128]{3,1,0,2:T(8,128)(2,1)S(1)} %get-tuple-element.14), channel_id=1, source_target_pairs={{0,4},{4,8},{8,12},{12,16},{16,20},{20,24},{24,28},{28,32},{32,36}... | collective-permute-start | bytes 393224 | tf_op jit(solution)/shard_map/ppermute | solution.py:12
  32.6 517.0 %reduce-scatter.2.cloned.1.call-start = ((), (), s32[]{:S(2)}) async-start(), calls=%async_computation.1 | async-start | bytes 2621440 | tf_op jit(solution)/shard_map/reduce_scatter | solution.py:89
  42.1 329.1 %collective-permute-start.1 = (bf16[1,256,2,128]{3,1,0,2:T(8,128)(2,1)S(1)}, bf16[1,256,2,128]{3,1,0,2:T(8,128)(2,1)S(1)}, u32[]{:S(2)}, u32[]{:S(2)}) collective-permute-start(bf16[1,256,2,128]{3,1,0,2:T(8,128)(2,1)S(1)} %get-tuple-element.9), channel_id=1, source_target_pairs={{0,8},{4,12},{8,16},{12,20},{16,24},{20,28},{24,32},{28,36},{32,40... | collective-permute-start | bytes 393224 | tf_op jit(solution)/shard_map/ppermute | solution.py:12
  365.9 9.7 %collective-permute-start.8 = (bf16[1,256,2,128]{3,1,0,2:T(8,128)(2,1)S(1)}, bf16[1,256,2,128]{3,1,0,2:T(8,128)(2,1)S(1)}, u32[]{:S(2)}, u32[]{:S(2)}) collective-permute-start(bf16[1,256,2,128]{3,1,0,2:T(8,128)(2,1)S(1)} %get-tuple-element.10), channel_id=1, source_target_pairs={{0,8},{4,12},{8,16},{12,20},{16,24},{20,28},{24,32},{28,36},{32,40... | collective-permute-start | bytes 393224 | tf_op jit(solution)/shard_map/ppermute | solution.py:12
  368.7 9.7 %collective-permute-start.15 = (bf16[1,256,2,128]{3,1,0,2:T(8,128)(2,1)S(1)}, bf16[1,256,2,128]{3,1,0,2:T(8,128)(2,1)S(1)}, u32[]{:S(2)}, u32[]{:S(2)}) collective-permute-start(bf16[1,256,2,128]{3,1,0,2:T(8,128)(2,1)S(1)} %get-tuple-element.11), channel_id=1, source_target_pairs={{0,8},{4,12},{8,16},{12,20},{16,24},{20,28},{24,32},{28,36},{32,40... | collective-permute-start | bytes 393224 | tf_op jit(solution)/shard_map/ppermute | solution.py:12
  371.2 11.7 %collective-permute-start.2 = (bf16[1,256,2,128]{3,1,0,2:T(8,128)(2,1)S(1)}, bf16[1,256,2,128]{3,1,0,2:T(8,128)(2,1)S(1)}, u32[]{:S(2)}, u32[]{:S(2)}) collective-permute-start(bf16[1,256,2,128]{3,1,0,2:T(8,128)(2,1)S(1)} %broadcast_select_fusion.20), channel_id=1, source_target_pairs={{0,16},{4,20},{8,24},{12,28},{16,32},{20,36},{24,40},{28,44},{32,4... | collective-permute-start | bytes 393224 | tf_op jit(solution)/shard_map/ppermute | solution.py:12
  375.7 11.5 %collective-permute-start.9 = (bf16[1,256,2,128]{3,1,0,2:T(8,128)(2,1)S(1)}, bf16[1,256,2,128]{3,1,0,2:T(8,128)(2,1)S(1)}, u32[]{:S(2)}, u32[]{:S(2)}) collective-permute-start(bf16[1,256,2,128]{3,1,0,2:T(8,128)(2,1)S(1)} %broadcast_select_fusion.13), channel_id=1, source_target_pairs={{0,16},{4,20},{8,24},{12,28},{16,32},{20,36},{24,40},{28,44},{32,4... | collective-permute-start | bytes 393224 | tf_op jit(solution)/shard_map/ppermute | solution.py:12
  378.5 10.6 %collective-permute-start.16 = (bf16[1,256,2,128]{3,1,0,2:T(8,128)(2,1)S(1)}, bf16[1,256,2,128]{3,1,0,2:T(8,128)(2,1)S(1)}, u32[]{:S(2)}, u32[]{:S(2)}) collective-permute-start(bf16[1,256,2,128]{3,1,0,2:T(8,128)(2,1)S(1)} %broadcast_select_fusion.6), channel_id=1, source_target_pairs={{0,16},{4,20},{8,24},{12,28},{16,32},{20,36},{24,40},{28,44},{32,4... | collective-permute-start | bytes 393224 | tf_op jit(solution)/shard_map/ppermute | solution.py:12
  382.9 8.9 %collective-permute-start.3 = (bf16[1,256,2,128]{3,1,0,2:T(8,128)(2,1)S(1)}, bf16[1,256,2,128]{3,1,0,2:T(8,128)(2,1)S(1)}, u32[]{:S(2)}, u32[]{:S(2)}) collective-permute-start(bf16[1,256,2,128]{3,1,0,2:T(8,128)(2,1)S(1)} %broadcast_select_fusion.21), channel_id=1, source_target_pairs={{0,32},{4,36},{8,40},{12,44},{16,48},{20,52},{24,56},{28,60},{32,6... | collective-permute-start | bytes 393224 | tf_op jit(solution)/shard_map/ppermute | solution.py:12
  387.2 10.2 %collective-permute-start.10 = (bf16[1,256,2,128]{3,1,0,2:T(8,128)(2,1)S(1)}, bf16[1,256,2,128]{3,1,0,2:T(8,128)(2,1)S(1)}, u32[]{:S(2)}, u32[]{:S(2)}) collective-permute-start(bf16[1,256,2,128]{3,1,0,2:T(8,128)(2,1)S(1)} %broadcast_select_fusion.14), channel_id=1, source_target_pairs={{0,32},{4,36},{8,40},{12,44},{16,48},{20,52},{24,56},{28,60},{32,6... | collective-permute-start | bytes 393224 | tf_op jit(solution)/shard_map/ppermute | solution.py:12
  389.2 10.8 %collective-permute-start.17 = (bf16[1,256,2,128]{3,1,0,2:T(8,128)(2,1)S(1)}, bf16[1,256,2,128]{3,1,0,2:T(8,128)(2,1)S(1)}, u32[]{:S(2)}, u32[]{:S(2)}) collective-permute-start(bf16[1,256,2,128]{3,1,0,2:T(8,128)(2,1)S(1)} %broadcast_select_fusion.7), channel_id=1, source_target_pairs={{0,32},{4,36},{8,40},{12,44},{16,48},{20,52},{24,56},{28,60},{32,6... | collective-permute-start | bytes 393224 | tf_op jit(solution)/shard_map/ppermute | solution.py:12
  391.9 12.1 %collective-permute-start.4 = (bf16[1,256,2,128]{3,1,0,2:T(8,128)(2,1)S(1)}, bf16[1,256,2,128]{3,1,0,2:T(8,128)(2,1)S(1)}, u32[]{:S(2)}, u32[]{:S(2)}) collective-permute-start(bf16[1,256,2,128]{3,1,0,2:T(8,128)(2,1)S(1)} %broadcast_select_fusion.22), channel_id=1, source_target_pairs={{0,64},{4,68},{8,72},{12,76},{16,80},{20,84},{24,88},{28,92},{32,9... | collective-permute-start | bytes 393224 | tf_op jit(solution)/shard_map/ppermute | solution.py:12
  397.4 10.5 %collective-permute-start.11 = (bf16[1,256,2,128]{3,1,0,2:T(8,128)(2,1)S(1)}, bf16[1,256,2,128]{3,1,0,2:T(8,128)(2,1)S(1)}, u32[]{:S(2)}, u32[]{:S(2)}) collective-permute-start(bf16[1,256,2,128]{3,1,0,2:T(8,128)(2,1)S(1)} %broadcast_select_fusion.15), channel_id=1, source_target_pairs={{0,64},{4,68},{8,72},{12,76},{16,80},{20,84},{24,88},{28,92},{32,9... | collective-permute-start | bytes 393224 | tf_op jit(solution)/shard_map/ppermute | solution.py:12
  400.0 14.0 %collective-permute-start.18 = (bf16[1,256,2,128]{3,1,0,2:T(8,128)(2,1)S(1)}, bf16[1,256,2,128]{3,1,0,2:T(8,128)(2,1)S(1)}, u32[]{:S(2)}, u32[]{:S(2)}) collective-permute-start(bf16[1,256,2,128]{3,1,0,2:T(8,128)(2,1)S(1)} %broadcast_select_fusion.8), channel_id=1, source_target_pairs={{0,64},{4,68},{8,72},{12,76},{16,80},{20,84},{24,88},{28,92},{32,9... | collective-permute-start | bytes 393224 | tf_op jit(solution)/shard_map/ppermute | solution.py:12
  404.0 14.2 %collective-permute-start.5 = (bf16[1,256,2,128]{3,1,0,2:T(8,128)(2,1)S(1)}, bf16[1,256,2,128]{3,1,0,2:T(8,128)(2,1)S(1)}, u32[]{:S(2)}, u32[]{:S(2)}) collective-permute-start(bf16[1,256,2,128]{3,1,0,2:T(8,128)(2,1)S(1)} %broadcast_select_fusion.23), channel_id=1, source_target_pairs={{0,128},{4,132},{8,136},{12,140},{16,144},{20,148},{24,152},{28,15... | collective-permute-start | bytes 393224 | tf_op jit(solution)/shard_map/ppermute | solution.py:12
  407.9 19.1 %collective-permute-start.12 = (bf16[1,256,2,128]{3,1,0,2:T(8,128)(2,1)S(1)}, bf16[1,256,2,128]{3,1,0,2:T(8,128)(2,1)S(1)}, u32[]{:S(2)}, u32[]{:S(2)}) collective-permute-start(bf16[1,256,2,128]{3,1,0,2:T(8,128)(2,1)S(1)} %broadcast_select_fusion.16), channel_id=1, source_target_pairs={{0,128},{4,132},{8,136},{12,140},{16,144},{20,148},{24,152},{28,15... | collective-permute-start | bytes 393224 | tf_op jit(solution)/shard_map/ppermute | solution.py:12
  414.0 18.3 %collective-permute-start.19 = (bf16[1,256,2,128]{3,1,0,2:T(8,128)(2,1)S(1)}, bf16[1,256,2,128]{3,1,0,2:T(8,128)(2,1)S(1)}, u32[]{:S(2)}, u32[]{:S(2)}) collective-permute-start(bf16[1,256,2,128]{3,1,0,2:T(8,128)(2,1)S(1)} %broadcast_select_fusion.9), channel_id=1, source_target_pairs={{0,128},{4,132},{8,136},{12,140},{16,144},{20,148},{24,152},{28,15... | collective-permute-start | bytes 393224 | tf_op jit(solution)/shard_map/ppermute | solution.py:12
  418.3 22.8 %collective-permute-start.6 = (bf16[1,256,2,128]{3,1,0,2:T(8,128)(2,1)S(1)}, bf16[1,256,2,128]{3,1,0,2:T(8,128)(2,1)S(1)}, u32[]{:S(2)}, u32[]{:S(2)}) collective-permute-start(bf16[1,256,2,128]{3,1,0,2:T(8,128)(2,1)S(1)} %broadcast_select_fusion.24), channel_id=1, source_target_pairs={{0,256},{4,260},{8,264},{12,268},{16,272},{20,276},{24,280},{28,28... | collective-permute-start | bytes 393224 | tf_op jit(solution)/shard_map/ppermute | solution.py:12
  427.0 24.1 %collective-permute-start.13 = (bf16[1,256,2,128]{3,1,0,2:T(8,128)(2,1)S(1)}, bf16[1,256,2,128]{3,1,0,2:T(8,128)(2,1)S(1)}, u32[]{:S(2)}, u32[]{:S(2)}) collective-permute-start(bf16[1,256,2,128]{3,1,0,2:T(8,128)(2,1)S(1)} %broadcast_select_fusion.17), channel_id=1, source_target_pairs={{0,256},{4,260},{8,264},{12,268},{16,272},{20,276},{24,280},{28,28... | collective-permute-start | bytes 393224 | tf_op jit(solution)/shard_map/ppermute | solution.py:12
  432.4 29.5 %collective-permute-start.20 = (bf16[1,256,2,128]{3,1,0,2:T(8,128)(2,1)S(1)}, bf16[1,256,2,128]{3,1,0,2:T(8,128)(2,1)S(1)}, u32[]{:S(2)}, u32[]{:S(2)}) collective-permute-start(bf16[1,256,2,128]{3,1,0,2:T(8,128)(2,1)S(1)} %broadcast_select_fusion.10), channel_id=1, source_target_pairs={{0,256},{4,260},{8,264},{12,268},{16,272},{20,276},{24,280},{28,28... | collective-permute-start | bytes 393224 | tf_op jit(solution)/shard_map/ppermute | solution.py:12
  468.9 5.8 %copy-start.1 = (bf16[1024,2048]{1,0:T(8,128)(2,1)S(1)}, bf16[1024,2048]{1,0:T(8,128)(2,1)}, u32[]{:S(2)}) copy-start(bf16[1024,2048]{1,0:T(8,128)(2,1)} %param.13) | copy-start | bytes 12582916
Sparse Core Ops, SparseCore 0:
  32.8 331.6 all-reduce.2
  477.4 72.1 reduce-scatter.1
where the time goes:
time: 559 us; the launch traced here: 558 us
  waiting for transfers between devices  413 us (74%)
  starting transfers between devices  86.4 us (15%)
  between operations  30.4 us (5%)
  matrix products  15.3 us (3%)
  other arithmetic  8.74 us (2%)
    psum x1, waiting for transfers between devices, broadcast(): return lax.psum(kept, axis)  319 us
    ppermute x21, starting transfers between devices, passed_along(): return lax.ppermute(value, axis, pairs)  86.4 us
    reduce_scatter x1, waiting for transfers between devices, body(): lax.psum_scatter(group_terms, 'head', scatter_dimension=1, tiled=True)  72.3 us
    ppermute x21, waiting for transfers between devices, passed_along(): return lax.ppermute(value, axis, pairs)  21.6 us
  transfers between devices with their start and end apart: 23, of which 5 were waited for; matrix products, arithmetic and copies ran while one was open for 2% of the time, Pallas kernels for 0%

commit v1 on v0

--- a/solution.py
+++ b/solution.py
@@ -14,7 +14,8 @@
 
 def broadcast(value, axis, source):
     kept = jnp.where(lax.axis_index(axis) == source, value, 0).astype(value.dtype)
-    return lax.psum(kept, axis)
+    see_tracks = lambda a0, comm_axis: jnp.sum(lax.all_gather(a0, comm_axis), axis=0)
+    return see_tracks(kept, axis)
 
 
 def rotate(stacked, amounts, shards):

time: 559 us -> 710 us (1.27)
  waiting for transfers between devices: 413 us -> 519 us
  other arithmetic: 8.74 us -> 42.9 us
  starting transfers between devices: 86.4 us -> 97.1 us
    all_gather x0 -> x4, waiting for transfers between devices: none -> 453 us  [broadcast(): lax.all_gather(a0, comm_axis)]
    psum x1 -> x0, waiting for transfers between devices: 319 us -> none  [broadcast(): return lax.psum(kept, axis)]
    reduce_scatter x1, waiting for transfers between devices: 72.3 us -> 32.2 us  [body(): lax.psum_scatter(group_terms, 'head', scatter_dimension=1, tiled=True)]
    reduce_sum x0 -> x4, other arithmetic: none -> 35 us  [broadcast(): jnp.sum(lax.all_gather(a0, comm_axis), axis=0)]
    ppermute x21, starting transfers between devices: 86.4 us -> 97 us  [passed_along(): return lax.ppermute(value, axis, pairs)]
    ppermute x21, waiting for transfers between devices: 21.6 us -> 31.6 us  [passed_along(): return lax.ppermute(value, axis, pairs)]
  transfers between devices with their start and end apart: 23 -> 26, of which waited for: 5 -> 11; matrix products, arithmetic and copies ran while one was open for 2% -> 5% of each run, Pallas kernels for 0% -> 0%
where the time goes in v1:
time: 710 us; the launch traced here: 709 us
  waiting for transfers between devices  519 us (73%)
  starting transfers between devices  97.1 us (14%)
  other arithmetic  42.9 us (6%)
  between operations  30.2 us (4%)
  matrix products  15.2 us (2%)
    all_gather x4, waiting for transfers between devices, broadcast(): lax.all_gather(a0, comm_axis)  453 us
    ppermute x21, starting transfers between devices, passed_along(): return lax.ppermute(value, axis, pairs)  97 us
    reduce_sum x4, other arithmetic, broadcast(): jnp.sum(lax.all_gather(a0, comm_axis), axis=0)  35 us
    reduce_scatter x1, waiting for transfers between devices, body(): lax.psum_scatter(group_terms, 'head', scatter_dimension=1, tiled=True)  32.2 us
    ppermute x21, waiting for transfers between devices, passed_along(): return lax.ppermute(value, axis, pairs)  31.6 us
  transfers between devices with their start and end apart: 26, of which 11 were waited for; matrix products, arithmetic and copies ran while one was open for 5% of the time, Pallas kernels for 0%

profile of v1, /device:TPU:1, one launch (start us, length us, event | category | flops | bytes accessed | tf_op | source)
XLA Modules:
  0.0 708.7 jit_solution(9513128308470783362)
XLA Ops:
  6.5 0.7 fusion.21
  7.3 0.7 fusion.26
  18.1 1.8 broadcast_select_fusion.4
  20.0 0.7 all-gather.11.cloned.1.call-update
  20.8 0.7 all-gather.15.cloned.1.call-update
  22.1 0.9 copy.22
  23.0 0.9 copy.24
  24.8 4.5 collective-permute-start
  29.3 1.9 collective-permute-start.14
  31.2 3.5 collective-permute-start.7
  36.4 1.4 fusion.25
  43.9 2.8 collective-permute-start.1
  47.6 3.5 collective-permute-start.8
  51.1 3.1 collective-permute-start.15
  54.2 3.1 collective-permute-done.1
  57.4 1.9 collective-permute-start.2
  59.3 1.5 collective-permute-done.8
  60.9 1.9 collective-permute-start.9
  62.8 1.0 collective-permute-done.15
  63.8 3.0 collective-permute-start.16
  66.9 3.5 collective-permute-start.3
  70.5 4.7 collective-permute-start.10
  75.3 3.5 collective-permute-start.17
  78.8 4.9 collective-permute-start.4
  83.8 6.3 collective-permute-start.11
  90.1 3.9 collective-permute-start.18
  94.0 5.6 collective-permute-start.5
  99.6 4.7 collective-permute-start.12
  104.3 7.0 collective-permute-start.19
  111.4 7.6 %collective-permute-start.6 = (bf16[1,256,2,128]{3,1,0,2:T(8,128)(2,1)S(1)}, bf16[1,256,2,128]{3,1,0,2:T(8,128)(2,1)S(1)}, u32[]{:S(2)}, u32[]{:S(2)}) collective-permute-start(bf16[1,256,2,128]{3,1,0,2:T(8,128)(2,1)S(1)} %broadcast_select_fusion.24), channel_id=1, source_target_pairs={{0,256},{4,260},{8,264},{12,268},{16,272},{20,276},{24,280},{28,28... | collective-permute-start | bytes 393224 | tf_op jit(solution)/shard_map/ppermute | solution.py:12
  119.0 7.4 %collective-permute-start.13 = (bf16[1,256,2,128]{3,1,0,2:T(8,128)(2,1)S(1)}, bf16[1,256,2,128]{3,1,0,2:T(8,128)(2,1)S(1)}, u32[]{:S(2)}, u32[]{:S(2)}) collective-permute-start(bf16[1,256,2,128]{3,1,0,2:T(8,128)(2,1)S(1)} %broadcast_select_fusion.17), channel_id=1, source_target_pairs={{0,256},{4,260},{8,264},{12,268},{16,272},{20,276},{24,280},{28,28... | collective-permute-start | bytes 393224 | tf_op jit(solution)/shard_map/ppermute | solution.py:12
  126.5 11.7 %collective-permute-start.20 = (bf16[1,256,2,128]{3,1,0,2:T(8,128)(2,1)S(1)}, bf16[1,256,2,128]{3,1,0,2:T(8,128)(2,1)S(1)}, u32[]{:S(2)}, u32[]{:S(2)}) collective-permute-start(bf16[1,256,2,128]{3,1,0,2:T(8,128)(2,1)S(1)} %broadcast_select_fusion.10), channel_id=1, source_target_pairs={{0,256},{4,260},{8,264},{12,268},{16,272},{20,276},{24,280},{28,28... | collective-permute-start | bytes 393224 | tf_op jit(solution)/shard_map/ppermute | solution.py:12
  138.2 1.4 collective-permute-done.6
  139.6 12.6 %collective-permute-done.13 = bf16[1,256,2,128]{3,1,0,2:T(8,128)(2,1)S(1)} collective-permute-done((bf16[1,256,2,128]{3,1,0,2:T(8,128)(2,1)S(1)}, bf16[1,256,2,128]{3,1,0,2:T(8,128)(2,1)S(1)}, u32[]{:S(2)}, u32[]{:S(2)}) %collective-permute-start.13) | collective-permute-done | bytes 131104 | tf_op jit(solution)/shard_map/ppermute | solution.py:12
  152.3 11.8 %collective-permute-done.20 = bf16[1,256,2,128]{3,1,0,2:T(8,128)(2,1)S(1)} collective-permute-done((bf16[1,256,2,128]{3,1,0,2:T(8,128)(2,1)S(1)}, bf16[1,256,2,128]{3,1,0,2:T(8,128)(2,1)S(1)}, u32[]{:S(2)}, u32[]{:S(2)}) %collective-permute-start.20) | collective-permute-done | bytes 131104 | tf_op jit(solution)/shard_map/ppermute | solution.py:12
  164.1 39.2 %all-gather.9.cloned.1.call-done = bf16[16384,2,128]{2,1,0:T(2,128)(2,1)} async-done(((bf16[128,2,128]{2,1,0:T(2,128)(2,1)}), bf16[16384,2,128]{2,1,0:T(2,128)(2,1)}) %all-gather.9.cloned.1.call-update) | async-done | bytes 8388624 | tf_op jit(solution)/shard_map/all_gather | solution.py:17
  203.3 8.7 %reduce_sum.57 = bf16[128,2,128]{2,1,0:T(2,128)(2,1)S(1)} reduce(bf16[128,128,2,128]{3,2,1,0:T(2,128)(2,1)} %bitcast.124, bf16[]{:T(256)} %constant.495.clone.1), dimensions={0}, to_apply=%region_0.1 | reduce | flops 4161536 | bytes 8454146 | tf_op jit(solution)/shard_map/reduce_sum | solution.py:17
  212.1 141.1 %all-gather.11.cloned.1.call-done = bf16[16384,2,128]{2,1,0:T(2,128)(2,1)} async-done(((bf16[128,2,128]{2,1,0:T(2,128)(2,1)}), bf16[16384,2,128]{2,1,0:T(2,128)(2,1)}) %all-gather.11.cloned.1.call-update) | async-done | bytes 8388624 | tf_op jit(solution)/shard_map/all_gather | solution.py:17
  353.2 8.7 %reduce_sum.58 = bf16[128,2,128]{2,1,0:T(2,128)(2,1)S(1)} reduce(bf16[128,128,2,128]{3,2,1,0:T(2,128)(2,1)} %bitcast.125, bf16[]{:T(256)} %constant.495.clone.1), dimensions={0}, to_apply=%region_1.2 | reduce | flops 4161536 | bytes 8454146 | tf_op jit(solution)/shard_map/reduce_sum | solution.py:17
  362.0 136.5 %all-gather.15.cloned.1.call-done = bf16[16384,2,128]{2,1,0:T(2,128)(2,1)} async-done(((bf16[128,2,128]{2,1,0:T(2,128)(2,1)}), bf16[16384,2,128]{2,1,0:T(2,128)(2,1)}) %all-gather.15.cloned.1.call-update) | async-done | bytes 8388624 | tf_op jit(solution)/shard_map/all_gather | solution.py:17
  498.4 8.7 %reduce_sum.60 = bf16[128,2,128]{2,1,0:T(2,128)(2,1)S(1)} reduce(bf16[128,128,2,128]{3,2,1,0:T(2,128)(2,1)} %bitcast.126, bf16[]{:T(256)} %constant.495.clone.1), dimensions={0}, to_apply=%region_3.4 | reduce | flops 4161536 | bytes 8454146 | tf_op jit(solution)/shard_map/reduce_sum | solution.py:17
  507.2 136.3 %all-gather.13.cloned.1.call-done = bf16[16384,2,128]{2,1,0:T(2,128)(2,1)} async-done(((bf16[128,2,128]{2,1,0:T(2,128)(2,1)}), bf16[16384,2,128]{2,1,0:T(2,128)(2,1)}) %all-gather.13.cloned.1.call-update) | async-done | bytes 8388624 | tf_op jit(solution)/shard_map/all_gather | solution.py:17
  643.5 8.7 %reduce_sum.59 = bf16[128,2,128]{2,1,0:T(2,128)(2,1)S(1)} reduce(bf16[128,128,2,128]{3,2,1,0:T(2,128)(2,1)} %bitcast.127, bf16[]{:T(256)} %constant.495.clone.1), dimensions={0}, to_apply=%region_2.3 | reduce | flops 4161536 | bytes 8454146 | tf_op jit(solution)/shard_map/reduce_sum | solution.py:17
  652.9 6.9 fusion.28
  659.8 5.7 fusion.8
  665.5 2.6 fusion.33
  668.2 32.2 %reduce-scatter.2.cloned.1.call-done = f32[256,512]{1,0:T(8,128)} async-done(((f32[256,2048]{1,0:T(8,128)}), f32[256,512]{1,0:T(8,128)}) %reduce-scatter.2.cloned.1.call-update) | async-done | bytes 524304 | tf_op jit(solution)/shard_map/reduce_scatter | solution.py:90
  700.4 1.8 convert_element_type.28
  (64 shorter events, 4.7 us)
Async XLA Ops:
  6.5 646.3 %copy-start = (bf16[256,1024]{1,0:T(8,128)(2,1)S(1)}, bf16[256,1024]{1,0:T(8,128)(2,1)}, u32[]{:S(2)}) copy-start(bf16[256,1024]{1,0:T(8,128)(2,1)} %param.7) | copy-start | bytes 1572868
  6.5 196.8 %all-gather.9.cloned.1.call-start = ((), (), s32[]{:S(2)}) async-start(), calls=%async_computation.2 | async-start | bytes 8454144 | tf_op jit(solution)/shard_map/all_gather | solution.py:17
  20.0 333.2 %all-gather.11.cloned.1.call-start = ((), (), s32[]{:S(2)}) async-start(), calls=%async_computation.3 | async-start | bytes 8454144 | tf_op jit(solution)/shard_map/all_gather | solution.py:17
  20.8 477.7 %all-gather.15.cloned.1.call-start = ((), (), s32[]{:S(2)}) async-start(), calls=%async_computation.5 | async-start | bytes 8454144 | tf_op jit(solution)/shard_map/all_gather | solution.py:17
  21.5 622.0 %all-gather.13.cloned.1.call-start = ((), (), s32[]{:S(2)}) async-start(), calls=%async_computation.4 | async-start | bytes 8454144 | tf_op jit(solution)/shard_map/all_gather | solution.py:17
  22.1 678.3 %reduce-scatter.2.cloned.1.call-start = ((), (), s32[]{:S(2)}) async-start(), calls=%async_computation.1 | async-start | bytes 2621440 | tf_op jit(solution)/shard_map/reduce_scatter | solution.py:90
  24.8 19.0 %collective-permute-start = (bf16[1,256,2,128]{3,1,0,2:T(8,128)(2,1)S(1)}, bf16[1,256,2,128]{3,1,0,2:T(8,128)(2,1)S(1)}, u32[]{:S(2)}, u32[]{:S(2)}) collective-permute-start(bf16[1,256,2,128]{3,1,0,2:T(8,128)(2,1)S(1)} %get-tuple-element.8), channel_id=1, source_target_pairs={{0,4},{4,8},{8,12},{12,16},{16,20},{20,24},{24,28},{28,32},{32,36}... | collective-permute-start | bytes 393224 | tf_op jit(solution)/shard_map/ppermute | solution.py:12
  29.3 14.5 %collective-permute-start.14 = (bf16[1,256,2,128]{3,1,0,2:T(8,128)(2,1)S(1)}, bf16[1,256,2,128]{3,1,0,2:T(8,128)(2,1)S(1)}, u32[]{:S(2)}, u32[]{:S(2)}) collective-permute-start(bf16[1,256,2,128]{3,1,0,2:T(8,128)(2,1)S(1)} %get-tuple-element.9), channel_id=1, source_target_pairs={{0,4},{4,8},{8,12},{12,16},{16,20},{20,24},{24,28},{28,32},{32,36}... | collective-permute-start | bytes 393224 | tf_op jit(solution)/shard_map/ppermute | solution.py:12
  31.2 12.6 %collective-permute-start.7 = (bf16[1,256,2,128]{3,1,0,2:T(8,128)(2,1)S(1)}, bf16[1,256,2,128]{3,1,0,2:T(8,128)(2,1)S(1)}, u32[]{:S(2)}, u32[]{:S(2)}) collective-permute-start(bf16[1,256,2,128]{3,1,0,2:T(8,128)(2,1)S(1)} %get-tuple-element.10), channel_id=1, source_target_pairs={{0,4},{4,8},{8,12},{12,16},{16,20},{20,24},{24,28},{28,32},{32,36}... | collective-permute-start | bytes 393224 | tf_op jit(solution)/shard_map/ppermute | solution.py:12
  43.9 13.5 %collective-permute-start.1 = (bf16[1,256,2,128]{3,1,0,2:T(8,128)(2,1)S(1)}, bf16[1,256,2,128]{3,1,0,2:T(8,128)(2,1)S(1)}, u32[]{:S(2)}, u32[]{:S(2)}) collective-permute-start(bf16[1,256,2,128]{3,1,0,2:T(8,128)(2,1)S(1)} %get-tuple-element.5), channel_id=1, source_target_pairs={{0,8},{4,12},{8,16},{12,20},{16,24},{20,28},{24,32},{28,36},{32,40... | collective-permute-start | bytes 393224 | tf_op jit(solution)/shard_map/ppermute | solution.py:12
  47.6 13.2 %collective-permute-start.8 = (bf16[1,256,2,128]{3,1,0,2:T(8,128)(2,1)S(1)}, bf16[1,256,2,128]{3,1,0,2:T(8,128)(2,1)S(1)}, u32[]{:S(2)}, u32[]{:S(2)}) collective-permute-start(bf16[1,256,2,128]{3,1,0,2:T(8,128)(2,1)S(1)} %get-tuple-element.6), channel_id=1, source_target_pairs={{0,8},{4,12},{8,16},{12,20},{16,24},{20,28},{24,32},{28,36},{32,40... | collective-permute-start | bytes 393224 | tf_op jit(solution)/shard_map/ppermute | solution.py:12
  51.1 12.7 %collective-permute-start.15 = (bf16[1,256,2,128]{3,1,0,2:T(8,128)(2,1)S(1)}, bf16[1,256,2,128]{3,1,0,2:T(8,128)(2,1)S(1)}, u32[]{:S(2)}, u32[]{:S(2)}) collective-permute-start(bf16[1,256,2,128]{3,1,0,2:T(8,128)(2,1)S(1)} %get-tuple-element.7), channel_id=1, source_target_pairs={{0,8},{4,12},{8,16},{12,20},{16,24},{20,28},{24,32},{28,36},{32,40... | collective-permute-start | bytes 393224 | tf_op jit(solution)/shard_map/ppermute | solution.py:12
  57.4 9.5 %collective-permute-start.2 = (bf16[1,256,2,128]{3,1,0,2:T(8,128)(2,1)S(1)}, bf16[1,256,2,128]{3,1,0,2:T(8,128)(2,1)S(1)}, u32[]{:S(2)}, u32[]{:S(2)}) collective-permute-start(bf16[1,256,2,128]{3,1,0,2:T(8,128)(2,1)S(1)} %broadcast_select_fusion.20), channel_id=1, source_target_pairs={{0,16},{4,20},{8,24},{12,28},{16,32},{20,36},{24,40},{28,44},{32,4... | collective-permute-start | bytes 393224 | tf_op jit(solution)/shard_map/ppermute | solution.py:12
  60.9 9.6 %collective-permute-start.9 = (bf16[1,256,2,128]{3,1,0,2:T(8,128)(2,1)S(1)}, bf16[1,256,2,128]{3,1,0,2:T(8,128)(2,1)S(1)}, u32[]{:S(2)}, u32[]{:S(2)}) collective-permute-start(bf16[1,256,2,128]{3,1,0,2:T(8,128)(2,1)S(1)} %broadcast_select_fusion.13), channel_id=1, source_target_pairs={{0,16},{4,20},{8,24},{12,28},{16,32},{20,36},{24,40},{28,44},{32,4... | collective-permute-start | bytes 393224 | tf_op jit(solution)/shard_map/ppermute | solution.py:12
  63.8 11.4 %collective-permute-start.16 = (bf16[1,256,2,128]{3,1,0,2:T(8,128)(2,1)S(1)}, bf16[1,256,2,128]{3,1,0,2:T(8,128)(2,1)S(1)}, u32[]{:S(2)}, u32[]{:S(2)}) collective-permute-start(bf16[1,256,2,128]{3,1,0,2:T(8,128)(2,1)S(1)} %broadcast_select_fusion.6), channel_id=1, source_target_pairs={{0,16},{4,20},{8,24},{12,28},{16,32},{20,36},{24,40},{28,44},{32,4... | collective-permute-start | bytes 393224 | tf_op jit(solution)/shard_map/ppermute | solution.py:12
  66.9 11.9 %collective-permute-start.3 = (bf16[1,256,2,128]{3,1,0,2:T(8,128)(2,1)S(1)}, bf16[1,256,2,128]{3,1,0,2:T(8,128)(2,1)S(1)}, u32[]{:S(2)}, u32[]{:S(2)}) collective-permute-start(bf16[1,256,2,128]{3,1,0,2:T(8,128)(2,1)S(1)} %broadcast_select_fusion.21), channel_id=1, source_target_pairs={{0,32},{4,36},{8,40},{12,44},{16,48},{20,52},{24,56},{28,60},{32,6... | collective-permute-start | bytes 393224 | tf_op jit(solution)/shard_map/ppermute | solution.py:12
  70.5 13.3 %collective-permute-start.10 = (bf16[1,256,2,128]{3,1,0,2:T(8,128)(2,1)S(1)}, bf16[1,256,2,128]{3,1,0,2:T(8,128)(2,1)S(1)}, u32[]{:S(2)}, u32[]{:S(2)}) collective-permute-start(bf16[1,256,2,128]{3,1,0,2:T(8,128)(2,1)S(1)} %broadcast_select_fusion.14), channel_id=1, source_target_pairs={{0,32},{4,36},{8,40},{12,44},{16,48},{20,52},{24,56},{28,60},{32,6... | collective-permute-start | bytes 393224 | tf_op jit(solution)/shard_map/ppermute | solution.py:12
  75.3 14.8 %collective-permute-start.17 = (bf16[1,256,2,128]{3,1,0,2:T(8,128)(2,1)S(1)}, bf16[1,256,2,128]{3,1,0,2:T(8,128)(2,1)S(1)}, u32[]{:S(2)}, u32[]{:S(2)}) collective-permute-start(bf16[1,256,2,128]{3,1,0,2:T(8,128)(2,1)S(1)} %broadcast_select_fusion.7), channel_id=1, source_target_pairs={{0,32},{4,36},{8,40},{12,44},{16,48},{20,52},{24,56},{28,60},{32,6... | collective-permute-start | bytes 393224 | tf_op jit(solution)/shard_map/ppermute | solution.py:12
  78.8 15.1 %collective-permute-start.4 = (bf16[1,256,2,128]{3,1,0,2:T(8,128)(2,1)S(1)}, bf16[1,256,2,128]{3,1,0,2:T(8,128)(2,1)S(1)}, u32[]{:S(2)}, u32[]{:S(2)}) collective-permute-start(bf16[1,256,2,128]{3,1,0,2:T(8,128)(2,1)S(1)} %broadcast_select_fusion.22), channel_id=1, source_target_pairs={{0,64},{4,68},{8,72},{12,76},{16,80},{20,84},{24,88},{28,92},{32,9... | collective-permute-start | bytes 393224 | tf_op jit(solution)/shard_map/ppermute | solution.py:12
  83.8 15.8 %collective-permute-start.11 = (bf16[1,256,2,128]{3,1,0,2:T(8,128)(2,1)S(1)}, bf16[1,256,2,128]{3,1,0,2:T(8,128)(2,1)S(1)}, u32[]{:S(2)}, u32[]{:S(2)}) collective-permute-start(bf16[1,256,2,128]{3,1,0,2:T(8,128)(2,1)S(1)} %broadcast_select_fusion.15), channel_id=1, source_target_pairs={{0,64},{4,68},{8,72},{12,76},{16,80},{20,84},{24,88},{28,92},{32,9... | collective-permute-start | bytes 393224 | tf_op jit(solution)/shard_map/ppermute | solution.py:12
  90.1 14.2 %collective-permute-start.18 = (bf16[1,256,2,128]{3,1,0,2:T(8,128)(2,1)S(1)}, bf16[1,256,2,128]{3,1,0,2:T(8,128)(2,1)S(1)}, u32[]{:S(2)}, u32[]{:S(2)}) collective-permute-start(bf16[1,256,2,128]{3,1,0,2:T(8,128)(2,1)S(1)} %broadcast_select_fusion.8), channel_id=1, source_target_pairs={{0,64},{4,68},{8,72},{12,76},{16,80},{20,84},{24,88},{28,92},{32,9... | collective-permute-start | bytes 393224 | tf_op jit(solution)/shard_map/ppermute | solution.py:12
  94.0 17.4 %collective-permute-start.5 = (bf16[1,256,2,128]{3,1,0,2:T(8,128)(2,1)S(1)}, bf16[1,256,2,128]{3,1,0,2:T(8,128)(2,1)S(1)}, u32[]{:S(2)}, u32[]{:S(2)}) collective-permute-start(bf16[1,256,2,128]{3,1,0,2:T(8,128)(2,1)S(1)} %broadcast_select_fusion.23), channel_id=1, source_target_pairs={{0,128},{4,132},{8,136},{12,140},{16,144},{20,148},{24,152},{28,15... | collective-permute-start | bytes 393224 | tf_op jit(solution)/shard_map/ppermute | solution.py:12
  99.6 19.4 %collective-permute-start.12 = (bf16[1,256,2,128]{3,1,0,2:T(8,128)(2,1)S(1)}, bf16[1,256,2,128]{3,1,0,2:T(8,128)(2,1)S(1)}, u32[]{:S(2)}, u32[]{:S(2)}) collective-permute-start(bf16[1,256,2,128]{3,1,0,2:T(8,128)(2,1)S(1)} %broadcast_select_fusion.16), channel_id=1, source_target_pairs={{0,128},{4,132},{8,136},{12,140},{16,144},{20,148},{24,152},{28,15... | collective-permute-start | bytes 393224 | tf_op jit(solution)/shard_map/ppermute | solution.py:12
  104.3 22.1 %collective-permute-start.19 = (bf16[1,256,2,128]{3,1,0,2:T(8,128)(2,1)S(1)}, bf16[1,256,2,128]{3,1,0,2:T(8,128)(2,1)S(1)}, u32[]{:S(2)}, u32[]{:S(2)}) collective-permute-start(bf16[1,256,2,128]{3,1,0,2:T(8,128)(2,1)S(1)} %broadcast_select_fusion.9), channel_id=1, source_target_pairs={{0,128},{4,132},{8,136},{12,140},{16,144},{20,148},{24,152},{28,15... | collective-permute-start | bytes 393224 | tf_op jit(solution)/shard_map/ppermute | solution.py:12
  111.4 28.2 %collective-permute-start.6 = (bf16[1,256,2,128]{3,1,0,2:T(8,128)(2,1)S(1)}, bf16[1,256,2,128]{3,1,0,2:T(8,128)(2,1)S(1)}, u32[]{:S(2)}, u32[]{:S(2)}) collective-permute-start(bf16[1,256,2,128]{3,1,0,2:T(8,128)(2,1)S(1)} %broadcast_select_fusion.24), channel_id=1, source_target_pairs={{0,256},{4,260},{8,264},{12,268},{16,272},{20,276},{24,280},{28,28... | collective-permute-start | bytes 393224 | tf_op jit(solution)/shard_map/ppermute | solution.py:12
  119.0 33.2 %collective-permute-start.13 = (bf16[1,256,2,128]{3,1,0,2:T(8,128)(2,1)S(1)}, bf16[1,256,2,128]{3,1,0,2:T(8,128)(2,1)S(1)}, u32[]{:S(2)}, u32[]{:S(2)}) collective-permute-start(bf16[1,256,2,128]{3,1,0,2:T(8,128)(2,1)S(1)} %broadcast_select_fusion.17), channel_id=1, source_target_pairs={{0,256},{4,260},{8,264},{12,268},{16,272},{20,276},{24,280},{28,28... | collective-permute-start | bytes 393224 | tf_op jit(solution)/shard_map/ppermute | solution.py:12
  126.5 37.6 %collective-permute-start.20 = (bf16[1,256,2,128]{3,1,0,2:T(8,128)(2,1)S(1)}, bf16[1,256,2,128]{3,1,0,2:T(8,128)(2,1)S(1)}, u32[]{:S(2)}, u32[]{:S(2)}) collective-permute-start(bf16[1,256,2,128]{3,1,0,2:T(8,128)(2,1)S(1)} %broadcast_select_fusion.10), channel_id=1, source_target_pairs={{0,256},{4,260},{8,264},{12,268},{16,272},{20,276},{24,280},{28,28... | collective-permute-start | bytes 393224 | tf_op jit(solution)/shard_map/ppermute | solution.py:12
  659.8 5.8 copy-start.1
Sparse Core Ops, SparseCore 0:
  20.1 183.1 all-gather.8
  206.5 146.6 all-gather.10
  356.4 142.0 all-gather.14
  501.4 142.0 all-gather.12
  668.3 32.0 reduce-scatter.1
